TPU v7x, 32 devices: a whole 2x2x4 slice. The times are simulated.
32 devices in a mesh: dp: 4 (over y, core), row: 2 (over x), col: 4 (over z).
Axes of the slice: x: 2, y: 2, z: 4, core: 2. Of those that a mesh axis runs over, the one named last changes fastest.
Arguments:
- tokens: bfloat16 [1024, 6144], P(('dp', 'col'), 'row'), may hold values from -6 to 6
- cotangent: bfloat16 [1024, 6144], P(('dp', 'col'), 'row'), may hold values from -6 to 6
- pre_act: bfloat16 [1024, 12288], P('dp', 'col'), may hold values from -6 to 6
- weight_in: bfloat16 [6144, 12288], P('row', 'col'), may hold values from -0.078125 to 0.078125
- weight_out: bfloat16 [12288, 6144], P('col', 'row'), may hold values from -0.0546875 to 0.0546875
Outputs:
- grad_tokens: bfloat16 [1024, 6144], P(('dp', 'col'), 'row')
- grad_in: float32 [6144, 12288], P('row', ('col', 'dp'))
- grad_out: float32 [12288, 6144], P(('col', 'dp'), 'row')
All inputs are finite; a program needn't handle non-finite values.
Results may differ from a plain program's by a relative error of at most 0.023.
Values may be sent and summed in bfloat16 or wider, within the bound.
A program may use at most 192 MiB of HBM per device.

v0:
```python
import jax
import jax.numpy as jnp
from jax import lax
from jax.sharding import PartitionSpec as P


def gelu_value(a):
    return 0.5 * a * (1.0 + lax.erf(a * 0.7071067811865476))


def gelu_slope(a):
    return (
        0.5 * (1.0 + lax.erf(a * 0.7071067811865476))
        + a * jnp.exp(-0.5 * a * a) * 0.3989422804014327
    )


def shards(tokens, cotangent, pre_act, weight_in, weight_out):
    contract = (((1,), (1,)), ((), ()))
    lead = (((0,), (0,)), ((), ()))
    tok_all, cot_all = (
        lax.all_gather(tokens, "col", axis=0, tiled=True),
        lax.all_gather(cotangent, "col", axis=0, tiled=True),
    )
    replica = tok_all.shape[0]
    total_tokens = replica * lax.axis_size("dp")
    factor = float(total_tokens) ** (-0.5)
    pre_float = pre_act.astype(jnp.float32)
    summed = lax.psum(
        lax.dot_general(cot_all, weight_out, contract, preferred_element_type=jnp.float32).astype(
            jnp.bfloat16
        ),
        "row",
    ).astype(jnp.float32)
    grad_pre = (summed * gelu_slope(pre_float)).astype(jnp.bfloat16)
    grad_tokens = lax.psum_scatter(
        lax.dot_general(grad_pre, weight_in, contract, preferred_element_type=jnp.float32).astype(
            jnp.bfloat16
        ),
        "col",
        scatter_dimension=0,
        tiled=True,
    )
    hidden = gelu_value(pre_float).astype(jnp.bfloat16)
    first = lax.dot_general(tok_all, grad_pre, lead, preferred_element_type=jnp.float32) * factor
    second = lax.dot_general(hidden, cot_all, lead, preferred_element_type=jnp.float32) * factor
    grad_in, grad_out = (
        lax.psum_scatter(first.astype(jnp.bfloat16), "dp", scatter_dimension=1, tiled=True).astype(
            jnp.float32
        ),
        lax.psum_scatter(second.astype(jnp.bfloat16), "dp", scatter_dimension=0, tiled=True).astype(
            jnp.float32
        ),
    )
    return (grad_tokens, grad_in, grad_out)


def solution(mesh):
    in_specs = (
        P(("dp", "col"), "row"),
        P(("dp", "col"), "row"),
        P("dp", "col"),
        P("row", "col"),
        P("col", "row"),
    )
    out_specs = (P(("dp", "col"), "row"), P("row", ("col", "dp")), P(("col", "dp"), "row"))
    return jax.shard_map(shards, mesh=mesh, in_specs=in_specs, out_specs=out_specs, check_vma=False)
```

profile of v0, /device:TPU:0, one launch (start us, length us, event | category | flops | bytes accessed | tf_op | source)
XLA Modules:
  0.0 469.2 jit_solution(8932405080684482068)
XLA Ops:
  7.2 0.0 all-gather.3.cloned.1.call-start
  7.2 0.7 all-gather.3.cloned.1.call-update
  7.9 0.0 all-gather.5.cloned.1.call-start
  7.9 0.7 all-gather.5.cloned.1.call-update
  8.6 0.0 copy-start
  8.7 0.0 all-reduce.2.cloned.1.call-start
  8.7 40.7 %all-gather.3.cloned.1.call-done = bf16[256,3072]{1,0:T(8,128)(2,1)} async-done(((bf16[64,3072]{1,0:T(8,128)(2,1)}), bf16[256,3072]{1,0:T(8,128)(2,1)}) %all-gather.3.cloned.1.call-update) | async-done | bytes 1572880 | tf_op jit(solution)/shard_map/all_gather | solution.py:23
  49.4 0.0 copy-start.2
  49.4 12.7 %convolution_convert_fusion.1 = bf16[256,3072]{1,0:T(8,128)(2,1)} fusion(bf16[256,3072]{1,0:T(8,128)(2,1)} %all-gather.3.cloned.1.call-done, bf16[3072,3072]{1,0:T(8,128)(2,1)} %param.9), kind=kOutput, calls=%fused_computation.9 | convolution fusion | flops 4832624640 | bytes 22020096 | tf_op jit(solution)/shard_map/dot_general | solution.py:30
  62.1 0.0 all-reduce.2.cloned.1.call-update
  62.1 0.0 reduce-scatter.8.cloned.1.call-start
  62.1 0.0 copy-done
  62.1 0.0 copy-done.2
  62.2 9.3 %multiply_convert_fusion = bf16[3072,3072]{1,0:T(8,128)(2,1)} fusion(bf16[256,3072]{1,0:T(8,128)(2,1)S(1)} %copy-done.2, bf16[256,3072]{1,0:T(8,128)(2,1)S(1)} %copy-done), kind=kOutput, calls=%fused_computation | convolution fusion | flops 4855431168 | bytes 22020096 | tf_op jit(solution)/shard_map/dot_general | solution.py:46
  71.5 0.0 reduce-scatter.8.cloned.1.call-update
  71.5 0.0 reduce-scatter.6.cloned.1.call-start
  71.5 15.4 %all-gather.5.cloned.1.call-done = bf16[256,3072]{1,0:T(8,128)(2,1)} async-done(((bf16[64,3072]{1,0:T(8,128)(2,1)}), bf16[256,3072]{1,0:T(8,128)(2,1)}) %all-gather.5.cloned.1.call-update) | async-done | bytes 1572880 | tf_op jit(solution)/shard_map/all_gather | solution.py:22
  86.9 53.3 %all-reduce.2.cloned.1.call-done = bf16[256,3072]{1,0:T(8,128)(2,1)} async-done(((bf16[256,3072]{1,0:T(8,128)(2,1)}), bf16[256,3072]{1,0:T(8,128)(2,1)}) %all-reduce.2.cloned.1.call-update) | async-done | bytes 1572880 | tf_op jit(solution)/shard_map/psum | solution.py:29
  140.2 13.6 %fusion = bf16[3072,3072]{0,1:T(8,128)(2,1)} fusion(bf16[256,3072]{1,0:T(8,128)(2,1)} %all-gather.5.cloned.1.call-done, bf16[256,3072]{1,0:T(8,128)(2,1)S(1)} %copy-done, bf16[256,3072]{1,0:T(8,128)(2,1)} %all-reduce.2.cloned.1.call-done), kind=kOutput, calls=%fused_computation.2 | convolution fusion | flops 4860149760 | bytes 23592960 | tf_op jit(solution)/shard_map/dot_general | solution.py:45
  153.8 0.0 copy-start.1
  153.8 0.0 reduce-scatter.6.cloned.1.call-update
  153.8 0.0 reduce-scatter.4.cloned.1.call-start
  153.9 1.8 copy-done.1
  155.7 14.6 %convolution_convert_fusion = bf16[256,3072]{1,0:T(8,128)(2,1)} fusion(bf16[3072,3072]{1,0:T(8,128)(2,1)} %param.8, bf16[256,3072]{1,0:T(8,128)(2,1)S(1)} %copy-done, bf16[256,3072]{1,0:T(8,128)(2,1)S(1)} %copy-done.1), kind=kOutput, calls=%fused_computation.8 | convolution fusion | flops 4842061824 | bytes 23592960 | tf_op jit(solution)/shard_map/dot_general | solution.py:37
  170.3 0.0 reduce-scatter.4.cloned.1.call-update
  170.3 112.0 %reduce-scatter.8.cloned.1.call-done = bf16[768,3072]{1,0:T(8,128)(2,1)} async-done(((bf16[3072,3072]{1,0:T(8,128)(2,1)}), bf16[768,3072]{1,0:T(8,128)(2,1)}) %reduce-scatter.8.cloned.1.call-update) | async-done | bytes 4718608 | tf_op jit(solution)/shard_map/reduce_scatter | solution.py:51
  282.2 7.4 %convert_element_type.43 = f32[768,3072]{1,0:T(8,128)} convert(bf16[768,3072]{1,0:T(8,128)(2,1)} %reduce-scatter.8.cloned.1.call-done) | non-fusion elementwise | flops 2359296 | bytes 14155776 | tf_op jit(solution)/shard_map/convert_element_type | solution.py:51
  289.6 134.6 %reduce-scatter.6.cloned.1.call-done = bf16[3072,768]{0,1:T(8,128)(2,1)} async-done(((bf16[3072,3072]{0,1:T(8,128)(2,1)}), bf16[3072,768]{0,1:T(8,128)(2,1)}) %reduce-scatter.6.cloned.1.call-update) | async-done | bytes 4718608 | tf_op jit(solution)/shard_map/reduce_scatter | solution.py:48
  424.2 7.4 %copy.8 = f32[3072,768]{1,0:T(8,128)} copy(bf16[3072,768]{0,1:T(8,128)(2,1)} %reduce-scatter.6.cloned.1.call-done) | data formatting | bytes 14155776
  431.6 30.8 %reduce-scatter.4.cloned.1.call-done = bf16[64,3072]{1,0:T(8,128)(2,1)} async-done(((bf16[256,3072]{1,0:T(8,128)(2,1)}), bf16[64,3072]{1,0:T(8,128)(2,1)}) %reduce-scatter.4.cloned.1.call-update) | async-done | bytes 393232 | tf_op jit(solution)/shard_map/reduce_scatter | solution.py:36
Async XLA Ops:
  7.2 42.2 %all-gather.3.cloned.1.call-start = ((), (), s32[]{:S(2)}) async-start(), calls=%async_computation.3 | async-start | bytes 1966080 | tf_op jit(solution)/shard_map/all_gather | solution.py:23
  7.9 79.1 %all-gather.5.cloned.1.call-start = ((), (), s32[]{:S(2)}) async-start(), calls=%async_computation.6 | async-start | bytes 1966080 | tf_op jit(solution)/shard_map/all_gather | solution.py:22
  8.6 53.5 %copy-start = (bf16[256,3072]{1,0:T(8,128)(2,1)S(1)}, bf16[256,3072]{1,0:T(8,128)(2,1)}, u32[]{:S(2)}) copy-start(bf16[256,3072]{1,0:T(8,128)(2,1)} %param.7) | copy-start | bytes 4718596
  8.7 131.5 %all-reduce.2.cloned.1.call-start = ((), (), s32[]{:S(2)}) async-start(), calls=%async_computation.4 | async-start | bytes 3145728 | tf_op jit(solution)/shard_map/psum | solution.py:29
  49.4 12.8 %copy-start.2 = (bf16[256,3072]{1,0:T(8,128)(2,1)S(1)}, bf16[256,3072]{1,0:T(8,128)(2,1)}, u32[]{:S(2)}) copy-start(bf16[256,3072]{1,0:T(8,128)(2,1)} %all-gather.3.cloned.1.call-done) | copy-start | bytes 4718596
  62.1 220.2 %reduce-scatter.8.cloned.1.call-start = ((), (), s32[]{:S(2)}) async-start(), calls=%async_computation.8 | async-start | bytes 23592960 | tf_op jit(solution)/shard_map/reduce_scatter | solution.py:51
  71.5 352.7 %reduce-scatter.6.cloned.1.call-start = ((), (), s32[]{:S(2)}) async-start(), calls=%async_computation.7 | async-start | bytes 23592960 | tf_op jit(solution)/shard_map/reduce_scatter | solution.py:48
  153.8 1.9 copy-start.1
  153.8 308.5 %reduce-scatter.4.cloned.1.call-start = ((), (), s32[]{:S(2)}) async-start(), calls=%async_computation.5 | async-start | bytes 1966080 | tf_op jit(solution)/shard_map/reduce_scatter | solution.py:36
Sparse Core Ops, SparseCore 0:
  9.6 39.7 all-gather.2
  51.0 35.9 all-gather.4
  89.8 50.3 all-reduce.1
  142.8 139.3 reduce-scatter.7
  284.7 139.4 reduce-scatter.5
  427.0 35.2 reduce-scatter.3
where the time goes:
time: 470 us; the launch traced here: 469 us
  waiting for transfers between devices  388 us (83%)
  matrix products  50.2 us (11%)
  between operations  14.1 us (3%)
  local copies, waits for them, and re-layouts  9.18 us (2%)
  other arithmetic  7.37 us (2%)
    reduce_scatter x1, waiting for transfers between devices, shards(): lax.psum_scatter(first.astype(jnp.bfloat16), 'dp', scatter_dimension=1, t...  135 us
    reduce_scatter x1, waiting for transfers between devices, shards(): lax.psum_scatter(second.astype(jnp.bfloat16), 'dp', scatter_dimension=0,...  112 us
    psum x1, waiting for transfers between devices, shards(): lax.psum(lax.dot_general(cot_all, weight_out, contract, preferred_element...  53.3 us
    all_gather x1, waiting for transfers between devices, shards(): lax.all_gather(cotangent, 'col', axis=0, tiled=True)  40.7 us
    reduce_scatter x1, waiting for transfers between devices, shards(): lax.psum_scatter(lax.dot_general(grad_pre, weight_in, contract, preferred...  30.8 us
    all_gather x1, waiting for transfers between devices, shards(): lax.all_gather(tokens, 'col', axis=0, tiled=True)  15.4 us
    dot_general x1, matrix products, shards(): lax.dot_general(grad_pre, weight_in, contract, preferred_element_type=jnp...  14.6 us
    dot_general x1, matrix products, shards(): lax.dot_general(tok_all, grad_pre, lead, preferred_element_type=jnp.float32)  13.6 us
  transfers between devices with their start and end apart: 6, of which 6 were waited for; matrix products, arithmetic and copies ran while one was open for 14% of the time, Pallas kernels for 0%

commit v1 on v0

--- a/solution.py
+++ b/solution.py
@@ -2,6 +2,28 @@
 import jax.numpy as jnp
 from jax import lax
 from jax.sharding import PartitionSpec as P
+
+
+def laid_out(pieces, dim):
+    pieces = jnp.moveaxis(pieces, 0, dim)
+    shape = pieces.shape
+    return pieces.reshape(*shape[:dim], shape[dim] * shape[dim + 1], *shape[dim + 2 :])
+
+
+def collect(shard, axis, dim):
+    devices = lax.axis_size(axis)
+    pairs = [(i, (i + 1) % devices) for i in range(devices)]
+    back = [(b, a) for a, b in pairs]
+    lower, upper = ([], [])
+    for lap in range(devices - 1):
+        if lap % 2 == 0:
+            lower.append(lax.ppermute(lower[-1] if lower else shard, axis, pairs))
+        else:
+            upper.append(lax.ppermute(upper[-1] if upper else shard, axis, back))
+    blocks = jnp.stack([*lower[::-1], shard, *upper])
+    shift = lax.axis_index(axis) - len(lower)
+    blocks = blocks[(jnp.arange(devices) - shift) % devices]
+    return laid_out(blocks, dim)
 
 
 def gelu_value(a):
@@ -20,7 +42,7 @@
     lead = (((0,), (0,)), ((), ()))
     tok_all, cot_all = (
         lax.all_gather(tokens, "col", axis=0, tiled=True),
-        lax.all_gather(cotangent, "col", axis=0, tiled=True),
+        collect(cotangent, "col", 0),
     )
     replica = tok_all.shape[0]
     total_tokens = replica * lax.axis_size("dp")

time: 470 us -> 433 us (0.921)
  waiting for transfers between devices: 388 us -> 345 us
  starting transfers between devices: 0.24 us -> 5.57 us
    all_gather x1 -> x0, waiting for transfers between devices: 40.7 us -> none  [shards(): lax.all_gather(cotangent, 'col', axis=0, tiled=True)]
    ppermute x0 -> x3, waiting for transfers between devices: none -> 26 us  [the longest x2 19 us: collect(): lower.append(lax.ppermute(lower[-1] if lower else shard, axis, pairs))]
    psum x1, waiting for transfers between devices: 53.3 us -> 35.4 us  [shards(): lax.psum(lax.dot_general(cot_all, weight_out, contract, preferred_element...]
    all_gather x1, waiting for transfers between devices: 15.4 us -> 5.9 us  [shards(): lax.all_gather(tokens, 'col', axis=0, tiled=True)]
    ppermute x0 -> x3, starting transfers between devices: none -> 5.17 us  [the longest x2 3.08 us: collect(): lower.append(lax.ppermute(lower[-1] if lower else shard, axis, pairs))]
  transfers between devices with their start and end apart: 6 -> 8, of which waited for: 6 -> 8; matrix products, arithmetic and copies ran while one was open for 14% -> 15% of each run, Pallas kernels for 0% -> 0%
where the time goes in v1:
time: 433 us; the launch traced here: 432 us
  waiting for transfers between devices  345 us (80%)
  matrix products  48.2 us (11%)
  between operations  15.7 us (4%)
  local copies, waits for them, and re-layouts  9.68 us (2%)
  other arithmetic  8.58 us (2%)
  starting transfers between devices  5.57 us (1%)
    reduce_scatter x1, waiting for transfers between devices, shards(): lax.psum_scatter(first.astype(jnp.bfloat16), 'dp', scatter_dimension=1, t...  134 us
    reduce_scatter x1, waiting for transfers between devices, shards(): lax.psum_scatter(second.astype(jnp.bfloat16), 'dp', scatter_dimension=0,...  112 us
    psum x1, waiting for transfers between devices, shards(): lax.psum(lax.dot_general(cot_all, weight_out, contract, preferred_element...  35.4 us
    reduce_scatter x1, waiting for transfers between devices, shards(): lax.psum_scatter(lax.dot_general(grad_pre, weight_in, contract, preferred...  30.9 us
    ppermute x2, waiting for transfers between devices, collect(): lower.append(lax.ppermute(lower[-1] if lower else shard, axis, pairs))  19 us
    dot_general x1, matrix products, shards(): lax.dot_general(grad_pre, weight_in, contract, preferred_element_type=jnp...  14.7 us
    dot_general x1, matrix products, shards(): lax.dot_general(tok_all, grad_pre, lead, preferred_element_type=jnp.float32)  13.7 us
    dot_general x1, matrix products, shards(): lax.dot_general(cot_all, weight_out, contract, preferred_element_type=jnp...  10.5 us
  transfers between devices with their start and end apart: 8, of which 8 were waited for; matrix products, arithmetic and copies ran while one was open for 15% of the time, Pallas kernels for 0%

profile of v1, /device:TPU:0, one launch (start us, length us, event | category | flops | bytes accessed | tf_op | source)
XLA Modules:
  0.0 432.4 jit_solution(3788232171868378292)
XLA Ops:
  8.0 0.0 all-gather.2.cloned.1.call-start
  8.0 3.1 collective-permute-start
  11.1 2.1 collective-permute-start.2
  13.2 10.1 %collective-permute-done = bf16[64,3072]{1,0:T(8,128)(2,1)S(1)} collective-permute-done((bf16[64,3072]{1,0:T(8,128)(2,1)}, bf16[64,3072]{1,0:T(8,128)(2,1)S(1)}, u32[]{:S(2)}, u32[]{:S(2)}) %collective-permute-start) | collective-permute-done | bytes 393248 | tf_op jit(solution)/shard_map/ppermute | solution.py:20
  23.3 0.0 collective-permute-start.1
  23.3 0.0 all-gather.2.cloned.1.call-update
  23.4 0.0 all-reduce.2.cloned.1.call-start
  23.5 7.1 %collective-permute-done.2 = bf16[64,3072]{1,0:T(8,128)(2,1)S(1)} collective-permute-done((bf16[64,3072]{1,0:T(8,128)(2,1)}, bf16[64,3072]{1,0:T(8,128)(2,1)S(1)}, u32[]{:S(2)}, u32[]{:S(2)}) %collective-permute-start.2) | collective-permute-done | bytes 393248 | tf_op jit(solution)/shard_map/ppermute | solution.py:22
  30.5 8.8 %collective-permute-done.1 = bf16[64,3072]{1,0:T(8,128)(2,1)S(1)} collective-permute-done((bf16[64,3072]{1,0:T(8,128)(2,1)S(1)}, bf16[64,3072]{1,0:T(8,128)(2,1)S(1)}, u32[]{:S(2)}, u32[]{:S(2)}) %collective-permute-start.1) | collective-permute-done | bytes 393248 | tf_op jit(solution)/shard_map/ppermute | solution.py:20
  39.4 1.2 pad_maximum_fusion
  40.6 0.6 gather_fusion
  41.2 0.0 copy-start
  41.2 10.5 %convolution_convert_fusion.1 = bf16[256,3072]{1,0:T(8,128)(2,1)} fusion(bf16[256,3072]{1,0:T(8,128)(2,1)S(1)} %bitcast.14, bf16[3072,3072]{1,0:T(8,128)(2,1)} %param.9), kind=kOutput, calls=%fused_computation.10 | convolution fusion | flops 4832624640 | bytes 22020096 | tf_op jit(solution)/shard_map/dot_general | solution.py:52
  51.7 0.0 all-reduce.2.cloned.1.call-update
  51.8 0.0 reduce-scatter.8.cloned.1.call-start
  51.8 0.0 copy-done
  51.8 9.3 %multiply_convert_fusion = bf16[3072,3072]{1,0:T(8,128)(2,1)} fusion(bf16[256,3072]{1,0:T(8,128)(2,1)S(1)} %bitcast.15, bf16[256,3072]{1,0:T(8,128)(2,1)S(1)} %copy-done), kind=kOutput, calls=%fused_computation.1 | convolution fusion | flops 4855431168 | bytes 22020096 | tf_op jit(solution)/shard_map/dot_general | solution.py:68
  61.2 0.0 reduce-scatter.8.cloned.1.call-update
  61.2 0.0 reduce-scatter.6.cloned.1.call-start
  61.3 5.9 %all-gather.2.cloned.1.call-done = bf16[256,3072]{1,0:T(8,128)(2,1)} async-done(((bf16[64,3072]{1,0:T(8,128)(2,1)}), bf16[256,3072]{1,0:T(8,128)(2,1)}) %all-gather.2.cloned.1.call-update) | async-done | bytes 1572880 | tf_op jit(solution)/shard_map/all_gather | solution.py:44
  67.2 35.4 %all-reduce.2.cloned.1.call-done = bf16[256,3072]{1,0:T(8,128)(2,1)} async-done(((bf16[256,3072]{1,0:T(8,128)(2,1)}), bf16[256,3072]{1,0:T(8,128)(2,1)}) %all-reduce.2.cloned.1.call-update) | async-done | bytes 1572880 | tf_op jit(solution)/shard_map/psum | solution.py:51
  102.5 13.7 %fusion = bf16[3072,3072]{0,1:T(8,128)(2,1)} fusion(bf16[256,3072]{1,0:T(8,128)(2,1)} %all-gather.2.cloned.1.call-done, bf16[256,3072]{1,0:T(8,128)(2,1)S(1)} %copy-done, bf16[256,3072]{1,0:T(8,128)(2,1)} %all-reduce.2.cloned.1.call-done), kind=kOutput, calls=%fused_computation.3 | convolution fusion | flops 4860149760 | bytes 23592960 | tf_op jit(solution)/shard_map/dot_general | solution.py:67
  116.2 0.0 copy-start.1
  116.2 0.0 reduce-scatter.6.cloned.1.call-update
  116.2 0.2 reduce-scatter.4.cloned.1.call-start
  116.5 1.6 copy-done.1
  118.1 14.7 %convolution_convert_fusion = bf16[256,3072]{1,0:T(8,128)(2,1)} fusion(bf16[3072,3072]{1,0:T(8,128)(2,1)} %param.8, bf16[256,3072]{1,0:T(8,128)(2,1)S(1)} %copy-done, bf16[256,3072]{1,0:T(8,128)(2,1)S(1)} %copy-done.1), kind=kOutput, calls=%fused_computation.9 | convolution fusion | flops 4842061824 | bytes 23592960 | tf_op jit(solution)/shard_map/dot_general | solution.py:59
  132.8 0.0 reduce-scatter.4.cloned.1.call-update
  132.8 111.8 %reduce-scatter.8.cloned.1.call-done = bf16[768,3072]{1,0:T(8,128)(2,1)} async-done(((bf16[3072,3072]{1,0:T(8,128)(2,1)}), bf16[768,3072]{1,0:T(8,128)(2,1)}) %reduce-scatter.8.cloned.1.call-update) | async-done | bytes 4718608 | tf_op jit(solution)/shard_map/reduce_scatter | solution.py:73
  244.6 7.4 %convert_element_type.43 = f32[768,3072]{1,0:T(8,128)} convert(bf16[768,3072]{1,0:T(8,128)(2,1)} %reduce-scatter.8.cloned.1.call-done) | non-fusion elementwise | flops 2359296 | bytes 14155776 | tf_op jit(solution)/shard_map/convert_element_type | solution.py:73
  252.0 134.5 %reduce-scatter.6.cloned.1.call-done = bf16[3072,768]{0,1:T(8,128)(2,1)} async-done(((bf16[3072,3072]{0,1:T(8,128)(2,1)}), bf16[3072,768]{0,1:T(8,128)(2,1)}) %reduce-scatter.6.cloned.1.call-update) | async-done | bytes 4718608 | tf_op jit(solution)/shard_map/reduce_scatter | solution.py:70
  386.5 7.4 %copy.8 = f32[3072,768]{1,0:T(8,128)} copy(bf16[3072,768]{0,1:T(8,128)(2,1)} %reduce-scatter.6.cloned.1.call-done) | data formatting | bytes 14155776
  393.9 30.9 %reduce-scatter.4.cloned.1.call-done = bf16[64,3072]{1,0:T(8,128)(2,1)} async-done(((bf16[256,3072]{1,0:T(8,128)(2,1)}), bf16[64,3072]{1,0:T(8,128)(2,1)}) %reduce-scatter.4.cloned.1.call-update) | async-done | bytes 393232 | tf_op jit(solution)/shard_map/reduce_scatter | solution.py:58
  (2 shorter events, 0.0 us)
Async XLA Ops:
  8.0 59.2 %all-gather.2.cloned.1.call-start = ((), (), s32[]{:S(2)}) async-start(), calls=%async_computation.5 | async-start | bytes 1966080 | tf_op jit(solution)/shard_map/all_gather | solution.py:44
  8.0 15.3 %collective-permute-start = (bf16[64,3072]{1,0:T(8,128)(2,1)}, bf16[64,3072]{1,0:T(8,128)(2,1)S(1)}, u32[]{:S(2)}, u32[]{:S(2)}) collective-permute-start(bf16[64,3072]{1,0:T(8,128)(2,1)} %param.6), channel_id=1, source_target_pairs={{0,1},{1,2},{2,3},{3,0},{4,5},{5,6},{6,7},{7,4},{8,9},{9,10},{10,1... | collective-permute-start | bytes 1179656 | tf_op jit(solution)/shard_map/ppermute | solution.py:20
  11.1 19.4 %collective-permute-start.2 = (bf16[64,3072]{1,0:T(8,128)(2,1)}, bf16[64,3072]{1,0:T(8,128)(2,1)S(1)}, u32[]{:S(2)}, u32[]{:S(2)}) collective-permute-start(bf16[64,3072]{1,0:T(8,128)(2,1)} %param.6), channel_id=1, source_target_pairs={{1,0},{2,1},{3,2},{0,3},{5,4},{6,5},{7,6},{4,7},{9,8},{10,9},{11,1... | collective-permute-start | bytes 1179656 | tf_op jit(solution)/shard_map/ppermute | solution.py:22
  23.3 16.0 %collective-permute-start.1 = (bf16[64,3072]{1,0:T(8,128)(2,1)S(1)}, bf16[64,3072]{1,0:T(8,128)(2,1)S(1)}, u32[]{:S(2)}, u32[]{:S(2)}) collective-permute-start(bf16[64,3072]{1,0:T(8,128)(2,1)S(1)} %collective-permute-done), channel_id=1, source_target_pairs={{0,1},{1,2},{2,3},{3,0},{4,5},{5,6},{6,7},{7,4},{8,9},{9,10},{10,1... | collective-permute-start | bytes 1179656 | tf_op jit(solution)/shard_map/ppermute | solution.py:20
  23.4 79.2 %all-reduce.2.cloned.1.call-start = ((), (), s32[]{:S(2)}) async-start(), calls=%async_computation.3 | async-start | bytes 3145728 | tf_op jit(solution)/shard_map/psum | solution.py:51
  41.2 10.6 %copy-start = (bf16[256,3072]{1,0:T(8,128)(2,1)S(1)}, bf16[256,3072]{1,0:T(8,128)(2,1)}, u32[]{:S(2)}) copy-start(bf16[256,3072]{1,0:T(8,128)(2,1)} %param.7) | copy-start | bytes 4718596
  51.8 192.8 %reduce-scatter.8.cloned.1.call-start = ((), (), s32[]{:S(2)}) async-start(), calls=%async_computation.7 | async-start | bytes 23592960 | tf_op jit(solution)/shard_map/reduce_scatter | solution.py:73
  61.2 325.3 %reduce-scatter.6.cloned.1.call-start = ((), (), s32[]{:S(2)}) async-start(), calls=%async_computation.6 | async-start | bytes 23592960 | tf_op jit(solution)/shard_map/reduce_scatter | solution.py:70
  116.2 1.9 copy-start.1
  116.2 308.6 %reduce-scatter.4.cloned.1.call-start = ((), (), s32[]{:S(2)}) async-start(), calls=%async_computation.4 | async-start | bytes 1966080 | tf_op jit(solution)/shard_map/reduce_scatter | solution.py:58
Sparse Core Ops, SparseCore 0:
  23.5 43.6 all-gather.1
Sparse Core Ops, SparseCore 1:
  51.9 50.6 all-reduce.1
  105.2 139.4 reduce-scatter.7
  247.1 139.3 reduce-scatter.5
  389.5 35.3 reduce-scatter.3
